TPU v7x, 32 devices: a whole 2x2x4 slice. The times are simulated.
32 devices in a mesh: rep: 2 (over y), dom: 16 (over z, x, core).
Axes of the slice: x: 2, y: 2, z: 4, core: 2. Of those that a mesh axis runs over, the one named last changes fastest.
Arguments:
- feats: bfloat16 [4096, 256], P(('rep', 'dom')), may hold values from -6 to 6
- w_self: bfloat16 [256, 256], replicated, may hold values from -0.375 to 0.375
- w_neigh: bfloat16 [256, 256], replicated, may hold values from -1.5 to 1.5
- tile_vals: bfloat16 [2, 16, 8, 128, 128], P('rep', 'dom'), may hold values from 0 to 1
- tile_owner: int32 [2, 16, 8], P('rep', 'dom'), may hold values from 0 to 15, as said below
- tile_src: int32 [2, 16, 8], P('rep', 'dom'), may hold values from 0 to 1
- tile_count: int32 [2, 16], P('rep', 'dom'), may hold values from 4 to 8, as said below
- d_out: bfloat16 [4096, 256], P(('rep', 'dom')), may hold values from -6 to 6
Outputs:
- out_feats: bfloat16 [4096, 256], P(('rep', 'dom'))
- d_feats: bfloat16 [4096, 256], P(('rep', 'dom'))
- grad_self: float32 [256, 256], P('dom')
- grad_neigh: float32 [256, 256], P('dom')
Inputs may be any that keep to these rules, and one draw needn't show every extreme that they name: Within one list no two tiles name the same pair of tile_owner and tile_src. Tiles of list (i, j) at positions tile_count[i, j] and beyond are padding.
All inputs are finite; a program needn't handle non-finite values.
Results may differ from a plain program's by a relative error of at most 0.0049.
Values may be sent and summed in bfloat16 or wider, within the bound.
A program may use at most 128 MiB of HBM per device.

v0:
```python
import functools

import jax
import jax.numpy as jnp
from jax import lax
from jax.experimental import pallas as pl
from jax.experimental.pallas import tpu as pltpu
from jax.sharding import PartitionSpec as P

F32 = jnp.float32
BF16 = jnp.bfloat16
MESH = pl.DeviceIdType.MESH
CUT = 48
EXTRA = 16


def dot(x, y):
    return jnp.dot(x, y, preferred_element_type=F32)


def dot_nt(x, y):
    return lax.dot_general(x, y, (((1,), (1,)), ((), ())), preferred_element_type=F32)


def dot_tn(x, y):
    return lax.dot_general(x, y, (((0,), (0,)), ((), ())), preferred_element_type=F32)


def kernel(
    dims,
    feats_in, w_self_in, w_neigh_in, tiles_in, owner_in, src_in, count_in, d_out_in,
    out_ref, d_feats_ref, g_self_ref, g_neigh_ref,
    feats_ref, w_self_ref, w_neigh_ref, tiles_ref, owner_ref, src_ref, count_ref, d_out_ref, load_s,
    panel, dense, dense_sib, dense_t, x_send, x_recv, own, own2, z_send, z_recv, z2_send, z2_recv, x2_send, x2_recv,
    gather, f_t, m_t, f_in, m_in, w_neigh_t, grad_acc, panel_acc, back_send, back_recv,
    gr_send, gr_recv,
    panel_s, panel_r, dense_s, dense_r, xs, xr, zs, zr, z2s, z2r, x2s, x2r, gzs, gzr, gxs, gxr, gcs, gcr,
    fs, fr, ms, mr, bs, br, grs, grr,
):
    R, A, B, T, hid, tiles, share, chunk, small = dims
    n_dom = A * B * 2
    rep = lax.axis_index("rep")
    dom = lax.axis_index("dom")
    c = lax.rem(dom, 2)
    b = lax.rem(lax.div(dom, 2), B)
    a = lax.div(dom, 2 * B)

    def dom_of(aa, bb, cc):
        return (aa * B + bb) * 2 + cc

    def plus(x, k, n):
        return lax.rem(x + k, n)

    sib = dom_of(a, b, 1 - c)

    def rcopy(src, dst, s, r, to_rep, to_dom):
        return pltpu.make_async_remote_copy(
            src_ref=src, dst_ref=dst, send_sem=s, recv_sem=r,
            device_id=(to_rep, to_dom), device_id_type=MESH,
        )

    barrier = pltpu.get_barrier_semaphore()
    for k in range(1, n_dom):
        pl.semaphore_signal(barrier, inc=1, device_id=(rep, plus(dom, k, n_dom)), device_id_type=MESH)
    for k in range(1, R):
        for cc in range(2):
            pl.semaphore_signal(
                barrier, inc=1, device_id=(plus(rep, k, R), dom_of(a, b, cc)), device_id_type=MESH
            )

    loads = []
    for i, (src, dst) in enumerate((
        (count_in, count_ref), (owner_in, owner_ref), (src_in, src_ref), (tiles_in, tiles_ref),
        (feats_in, feats_ref), (w_self_in, w_self_ref), (w_neigh_in, w_neigh_ref),
        (d_out_in, d_out_ref),
    )):
        cp = pltpu.make_async_copy(src, dst, load_s.at[i])
        cp.start()
        loads.append(cp)
    for cp in loads[:4]:
        cp.wait()

    keys = None
    if small:
        keys = [
            jnp.where(t < count_ref[0, 0], owner_ref[t] * R + src_ref[t], -1) for t in range(tiles)
        ]

    def place(pair):
        if small:
            at, live = jnp.int32(0), jnp.int32(0)
            for t in range(tiles):
                hit = keys[t] == pair
                at = jnp.where(hit, t, at)
                live = jnp.where(hit, 1, live)
            return at, live

        def look(t, state):
            hit = (owner_ref[t] * R + src_ref[t] == pair) & (t < count_ref[0, 0])
            return jnp.where(hit, t, state[0]), jnp.where(hit, 1, state[1])

        return lax.fori_loop(0, tiles, look, (jnp.int32(0), jnp.int32(0)))

    def build(cc, bb):
        def one(aa, _):
            d = dom_of(aa, bb, cc)
            for s in range(R):
                at, live = place(d * R + s)
                mask = jnp.full((T, T), live.astype(F32), F32).astype(BF16)
                dense[cc, bb, aa, :, s * T:(s + 1) * T] = tiles_ref[at] * mask
            return 0
        if small:
            for aa in range(A):
                one(aa, 0)
        else:
            lax.fori_loop(0, A, one, 0)

    for kb in list(range(1, B)) + [0]:
        build(1 - c, plus(b, kb, B))

    for cp in loads[4:]:
        cp.wait()
    f_t[...] = feats_ref[...].T
    panel[c, pl.ds(pl.multiple_of(rep * T, T), T), :] = feats_ref[...]

    pl.semaphore_wait(barrier, n_dom - 1 + 2 * (R - 1))

    copies = []
    panel_in = []
    for kr in range(R):
        for kc in range(2):
            if kr == 0 and kc == 0:
                continue
            to_c = plus(c, kc, 2)
            cp = rcopy(
                feats_ref, panel.at[c, pl.ds(pl.multiple_of(rep * T, T), T)],
                panel_s.at[kr * 2 + kc], panel_r.at[kr * 2 + kc], plus(rep, R - kr, R),
                dom_of(a, b, to_c),
            )
            cp.start()
            copies.append(cp)
            panel_in.append(cp)
    dense_in = {}
    for kb in list(range(1, B)) + [0]:
        bb = plus(b, kb, B)
        cp = rcopy(dense.at[1 - c, bb], dense_sib.at[bb], dense_s.at[kb], dense_r.at[kb], rep, sib)
        cp.start()
        copies.append(cp)
        dense_in[kb] = cp

    def scatter(src, dst, s, r):
        for k in range(1, n_dom):
            to = plus(dom, k, n_dom)
            row = pl.multiple_of(lax.div(to * share, chunk) * chunk, chunk)
            cp = rcopy(src.at[pl.ds(row, chunk)], dst.at[dom], s.at[k], r.at[k], rep, to)
            cp.start()
            copies.append(cp)
        row = pl.multiple_of(lax.div(dom * share, chunk) * chunk, chunk)
        dst[dom] = src[pl.ds(row, chunk), :]

    def scatter_wait(src, dst, s, r):
        for k in range(1, n_dom):
            frm = plus(dom, n_dom - k, n_dom)
            rcopy(src.at[pl.ds(0, chunk)], dst.at[frm], s.at[k], r.at[k], rep, frm).wait_recv()

    scatter(f_t, f_in, fs, fr)
    for kb in list(range(1, B)) + [0]:
        build(c, plus(b, kb, B))

    ones = jnp.ones((EXTRA, R * T), BF16)

    def block_sum(bb, aa):
        top = dot(dense[c, bb, aa], panel[c]) + dot(dense_sib[bb, aa], panel[1 - c])
        deg = dot_nt(ones, dense[c, bb, aa]) + dot_nt(ones, dense_sib[bb, aa])
        return top, deg

    def pack(dst, top, row):
        n = top.shape[0]
        high = row.astype(BF16)
        dst[0:n, :] = top.astype(BF16)
        dst[n:n + EXTRA, 0:T] = high
        dst[n:n + EXTRA, T:2 * T] = (row - high.astype(F32)).astype(BF16)

    for cp in panel_in:
        cp.wait_recv()
    order = [2, 3, 1, 0] if A == 4 else list(range(1, A)) + [0]
    for kb in range(B):
        dense_in[kb].wait_recv()
    for ka in order:
        aa = plus(a, ka, A)
        for kb in list(range(1, B)) + [0]:
            bb = plus(b, kb, B)
            top, deg = block_sum(bb, aa)
            if ka > 0:
                z2_send[ka, kb * CUT:(kb + 1) * CUT, :] = top[0:CUT].astype(BF16)
            else:
                own2[kb] = top[0:CUT]
            if kb > 0:
                pack(x_send.at[kb - 1, ka], top[CUT:], deg)
                i = (kb - 1) * A + ka
                cp = rcopy(x_send.at[kb - 1, ka], x_recv.at[kb - 1, ka], xs.at[i], xr.at[i], rep,
                           dom_of(a, bb, c))
                cp.start()
                copies.append(cp)
            else:
                own[ka, 0:T - CUT, :] = top[CUT:]
                own[ka, T - CUT:T - CUT + EXTRA, 0:T] = deg
        if ka > 0:
            cp = rcopy(z2_send.at[ka], z2_recv.at[ka], z2s.at[ka], z2r.at[ka], rep, dom_of(aa, b, c))
            cp.start()
            copies.append(cp)

    low = T - CUT

    def with_x(ka):
        top = own[ka, 0:low, :]
        deg = own[ka, low:low + EXTRA, 0:T]
        for kb in range(1, B):
            i = (kb - 1) * A + ka
            rcopy(x_send.at[kb - 1, ka], x_recv.at[kb - 1, ka], xs.at[i], xr.at[i], rep, sib).wait_recv()
            got = x_recv[kb - 1, ka].astype(F32)
            top = top + got[0:low]
            deg = deg + got[low:, 0:T] + got[low:, T:2 * T]
        return top, deg

    for ka in order[:-1]:
        top, deg = with_x(ka)
        pack(z_send.at[ka], top, deg)
        cp = rcopy(z_send.at[ka], z_recv.at[ka], zs.at[ka], zr.at[ka], rep,
                   dom_of(plus(a, ka, A), b, c))
        cp.start()
        copies.append(cp)
    for ka in order[:-1]:
        rcopy(z2_send.at[ka], z2_recv.at[ka], z2s.at[ka], z2r.at[ka], rep, sib).wait_recv()
    for kb in list(range(1, B)) + [0]:
        part = own2[kb]
        for ka in range(1, A):
            part = part + z2_recv[ka, kb * CUT:(kb + 1) * CUT, :].astype(F32)
        if kb > 0:
            x2_send[kb] = part.astype(BF16)
            cp = rcopy(x2_send.at[kb], x2_recv.at[kb], x2s.at[kb], x2r.at[kb], rep,
                       dom_of(a, plus(b, kb, B), c))
            cp.start()
            copies.append(cp)
    head = part

    w_neigh_t[...] = w_neigh_ref[...].T
    pre_self = dot(feats_ref[...], w_self_ref[...])
    if small:
        for aa in range(A):
            for bb in range(B):
                for cc in range(2):
                    dense_t[aa, bb, :, cc * T:(cc + 1) * T] = dense[cc, bb, aa].T

    top, deg = with_x(0)
    for ka in order[:-1]:
        rcopy(z_send.at[ka], z_recv.at[ka], zs.at[ka], zr.at[ka], rep, sib).wait_recv()
        got = z_recv[ka].astype(F32)
        top = top + got[0:low]
        deg = deg + got[low:, 0:T] + got[low:, T:2 * T]
    for kb in range(1, B):
        rcopy(x2_send.at[kb], x2_recv.at[kb], x2s.at[kb], x2r.at[kb], rep, sib).wait_recv()
        head = head + x2_recv[kb].astype(F32)
    top = jnp.concatenate([head, top], axis=0)

    inv = 1.0 / (1.0 + deg)

    def as_column(row):
        col = jnp.broadcast_to(row[0:1, :], (T, T)).T
        return jnp.concatenate([col] * (hid // T), axis=1)

    mean = (top * as_column(inv)).astype(BF16)
    pre = pre_self + dot(mean, w_neigh_ref[...])
    g = jax.nn.sigmoid(pre)
    d_pre = (d_out_ref[...].astype(F32) * g * (1.0 + pre * (1.0 - g))).astype(BF16)
    mine = gather.at[a, b, c]
    pack(mine, d_pre, inv)

    def send_a(ka):
        cp = rcopy(mine, mine, gzs.at[ka], gzr.at[ka], rep, dom_of(plus(a, ka, A), b, c))
        cp.start()
        copies.append(cp)

    def block_at(ka, kb, cc):
        return gather.at[plus(a, A - ka, A), plus(b, B - kb, B), cc]

    def send_b(ka):
        blk = block_at(ka, 0, c)
        for kb in range(1, B):
            i = kb * A + ka
            cp = rcopy(blk, blk, gxs.at[i], gxr.at[i], rep, dom_of(a, plus(b, kb, B), c))
            cp.start()
            copies.append(cp)

    def send_c(ka, kb):
        blk = block_at(ka, kb, c)
        i = kb * A + ka
        cp = rcopy(blk, blk, gcs.at[i], gcr.at[i], rep, sib)
        cp.start()
        copies.append(cp)

    early = copies[:]
    copies.clear()
    for ka in order[:-1]:
        send_a(ka)
    send_b(0)
    send_c(0, 0)
    out_ref[...] = (pre * g).astype(BF16)
    m_t[...] = mean.T
    d_self = dot_nt(d_pre, w_self_ref[...])
    for ec in early:
        ec.wait_send()
    panel_acc[...] = jnp.zeros_like(panel_acc)
    grad_acc[...] = jnp.zeros_like(grad_acc)
    scatter(m_t, m_in, ms, mr)

    def wait_c(ka, kb):
        blk = block_at(ka, kb, 1 - c)
        i = kb * A + ka
        rcopy(blk, blk, gcs.at[i], gcr.at[i], rep, sib).wait_recv()

    def use_pair(ka, kb):
        wait_c(ka, kb)
        aa, bb = plus(a, A - ka, A), plus(b, B - kb, B)
        d = [gather[aa, bb, cc, 0:T, :] for cc in range(2)]
        both = jnp.concatenate(d, axis=0)
        cols = []
        for cc in range(2):
            row = gather[aa, bb, cc, T:T + EXTRA, :].astype(F32)
            cols.append(as_column(row[:, 0:T] + row[:, T:2 * T]))
        d_sum = (dot(both, w_neigh_t[...]) * jnp.concatenate(cols, axis=0)).astype(BF16)
        if small:
            panel_acc[...] += dot(dense_t[aa, bb], d_sum)
        else:
            for cc in range(2):
                for s in range(R):
                    panel_acc[s * T:(s + 1) * T, :] += dot_tn(
                        dense[cc, bb, aa, :, s * T:(s + 1) * T], d_sum[cc * T:(cc + 1) * T]
                    )

    def grads_of(ka, kb):
        aa, bb = plus(a, A - ka, A), plus(b, B - kb, B)
        first = dom_of(aa, bb, 0)
        lhs = [jnp.concatenate([r[first], r[first + 1]], axis=1) for r in (f_in, m_in)]
        rhs = jnp.concatenate([gather[aa, bb, cc, 0:T, :] for cc in range(2)], axis=0)
        grad_acc[...] += dot(jnp.concatenate(lhs, axis=0), rhs)

    done = []
    later = []
    for ka in [0] + order[:-1]:
        if ka > 0:
            blk = block_at(ka, 0, c)
            rcopy(blk, blk, gzs.at[ka], gzr.at[ka], rep, sib).wait_recv()
            send_b(ka)
            send_c(ka, 0)
        for kb in range(1, B):
            blk = block_at(ka, kb, c)
            i = kb * A + ka
            rcopy(blk, blk, gxs.at[i], gxr.at[i], rep, sib).wait_recv()
            send_c(ka, kb)
        for pair in later:
            use_pair(*pair)
        done += later
        later = [(ka, kb) for kb in range(B)]
    use_pair(*later[0])
    done.append(later.pop(0))
    scatter_wait(f_t, f_in, fs, fr)
    scatter_wait(m_t, m_in, ms, mr)
    for pair in done:
        grads_of(*pair)
    for pair in later:
        use_pair(*pair)

    back = []
    for kr in range(1, R):
        to = plus(rep, kr, R)
        rows = pl.ds(pl.multiple_of(to * T, T), T)
        back_send[kr] = panel_acc[rows, :].astype(BF16)
        cp = rcopy(back_send.at[kr], back_recv.at[kr], bs.at[kr], br.at[kr], to, dom)
        cp.start()
        back.append(cp)
    for pair in later:
        grads_of(*pair)
    gr_send[...] = grad_acc[...]
    for kr in range(1, R):
        cp = rcopy(gr_send, gr_recv.at[kr], grs.at[kr], grr.at[kr], plus(rep, kr, R), dom)
        cp.start()
        back.append(cp)
    for cp in copies:
        cp.wait_send()

    mine_rows = pl.ds(pl.multiple_of(rep * T, T), T)
    total = d_self + panel_acc[mine_rows, :]
    for kr in range(1, R):
        back[kr - 1].wait_recv()
        total = total + back_recv[kr].astype(F32)
    d_feats_ref[...] = total.astype(BF16)
    grads = grad_acc[...]
    for kr in range(1, R):
        back[R - 1 + kr - 1].wait_recv()
        grads = grads + gr_recv[kr]
    at = lax.rem(dom * share, chunk)
    for i, ref in enumerate((g_self_ref, g_neigh_ref)):
        part = grads[i * chunk:(i + 1) * chunk]
        res = part[0:share]
        for k in range(1, chunk // share):
            res = jnp.where(at == k * share, part[k * share:(k + 1) * share], res)
        ref[...] = res

    for cp in back:
        cp.wait_send()


def finish(*refs):
    n = (len(refs) - 1) // 2
    sems = refs[-1]
    moves = [pltpu.make_async_copy(refs[i], refs[n + i], sems.at[i]) for i in range(n)]
    for cp in moves:
        cp.start()
    for cp in moves:
        cp.wait()


def per_device(feats, w_self, w_neigh, tile_vals, tile_owner, tile_src, tile_count, d_out):
    R = lax.axis_size("rep")
    n_dom = lax.axis_size("dom")
    A = 4
    B = n_dom // (2 * A)
    T, hid = feats.shape
    tiles = tile_vals.shape[2]
    share = hid // n_dom
    chunk = max(share, 16)
    small = tiles <= 16
    msg = T + EXTRA
    dims = (R, A, B, T, hid, tiles, share, chunk, small)
    vmem = pl.BlockSpec(memory_space=pltpu.VMEM)
    anywhere = pl.BlockSpec(memory_space=pl.ANY)
    dma = pltpu.SemaphoreType.DMA
    scratch = [
        pltpu.VMEM((T, hid), BF16),
        pltpu.VMEM((hid, hid), BF16),
        pltpu.VMEM((hid, hid), BF16),
        pltpu.VMEM((tiles, T, T), BF16),
        pltpu.SMEM((tiles,), jnp.int32),
        pltpu.SMEM((tiles,), jnp.int32),
        pltpu.SMEM((1, 1), jnp.int32),
        pltpu.VMEM((T, hid), BF16),
        dma((8,)),
        pltpu.VMEM((2, R * T, hid), BF16),
        pltpu.VMEM((2, B, A, T, R * T), BF16),
        pltpu.VMEM((B, A, T, R * T), BF16),
        pltpu.VMEM((A, B, R * T, 2 * T) if small else (1, 1, 16, 128), BF16),
        pltpu.VMEM((B - 1, A, msg - CUT, hid), BF16),
        pltpu.VMEM((B - 1, A, msg - CUT, hid), BF16),
        pltpu.VMEM((A, msg - CUT, hid), F32),
        pltpu.VMEM((B, CUT, hid), F32),
        pltpu.VMEM((A, msg - CUT, hid), BF16),
        pltpu.VMEM((A, msg - CUT, hid), BF16),
        pltpu.VMEM((A, B * CUT, hid), BF16),
        pltpu.VMEM((A, B * CUT, hid), BF16),
        pltpu.VMEM((B, CUT, hid), BF16),
        pltpu.VMEM((B, CUT, hid), BF16),
        pltpu.VMEM((A, B, 2, msg, hid), BF16),
        pltpu.VMEM((hid, T), BF16),
        pltpu.VMEM((hid, T), BF16),
        pltpu.VMEM((n_dom, chunk, T), BF16),
        pltpu.VMEM((n_dom, chunk, T), BF16),
        pltpu.VMEM((hid, hid), BF16),
        pltpu.VMEM((2 * chunk, hid), F32),
        pltpu.VMEM((R * T, hid), F32),
        pltpu.VMEM((R, T, hid), BF16),
        pltpu.VMEM((R, T, hid), BF16),
        pltpu.VMEM((2 * chunk, hid), F32),
        pltpu.VMEM((R, 2 * chunk, hid), F32),
        dma((2 * R,)), dma((2 * R,)),
        dma((B,)), dma((B,)),
        dma(((B - 1) * A,)), dma(((B - 1) * A,)),
        dma((A,)), dma((A,)),
        dma((A,)), dma((A,)),
        dma((B,)), dma((B,)),
        dma((A,)), dma((A,)),
        dma((A * B,)), dma((A * B,)),
        dma((A * B,)), dma((A * B,)),
        dma((n_dom,)), dma((n_dom,)),
        dma((n_dom,)), dma((n_dom,)),
        dma((R,)), dma((R,)),
        dma((R,)), dma((R,)),
    ]
    results = pl.pallas_call(
        functools.partial(kernel, dims),
        out_shape=(
            pltpu.VMEM((T, hid), BF16),
            pltpu.VMEM((T, hid), BF16),
            pltpu.VMEM((share, hid), F32),
            pltpu.VMEM((share, hid), F32),
        ),
        in_specs=[anywhere] * 8,
        out_specs=(vmem, vmem, vmem, vmem),
        scratch_shapes=scratch,
        compiler_params=pltpu.CompilerParams(
            collective_id=0, has_side_effects=True, vmem_limit_bytes=60 * 1024 * 1024
        ),
        name="sage_layer",
    )(
        feats, w_self, w_neigh, tile_vals[0, 0], tile_owner.reshape(-1), tile_src.reshape(-1),
        tile_count, d_out,
    )
    return pl.pallas_call(
        finish,
        out_shape=tuple(jax.ShapeDtypeStruct(r.shape, r.dtype) for r in results),
        in_specs=[vmem] * 4,
        out_specs=(anywhere,) * 4,
        scratch_shapes=[dma((4,))],
        compiler_params=pltpu.CompilerParams(vmem_limit_bytes=1024 * 1024),
        name="place_results",
    )(*results)


def solution(mesh):
    in_specs = (
        P(("rep", "dom"), None),
        P(),
        P(),
        P("rep", "dom", None, None, None),
        P("rep", "dom", None),
        P("rep", "dom", None),
        P("rep", "dom"),
        P(("rep", "dom"), None),
    )
    out_specs = (P(("rep", "dom"), None), P(("rep", "dom"), None), P("dom", None), P("dom", None))
    return jax.shard_map(
        per_device, mesh=mesh, in_specs=in_specs, out_specs=out_specs, check_vma=False
    )
```

profile of v0, /device:TPU:0, one launch (start us, length us, event | category | flops | bytes accessed | tf_op | source)
XLA Modules:
  0.0 49.9 jit_solution(7872573516223683681)
XLA Ops:
  1.3 48.0 %sage_layer.1 = (bf16[128,256]{1,0:T(8,128)(2,1)S(1)}, bf16[128,256]{1,0:T(8,128)(2,1)S(1)}, f32[16,256]{1,0:T(8,128)S(1)}, f32[16,256]{1,0:T(8,128)S(1)}) custom-call(bf16[128,256]{1,0:T(8,128)(2,1)} %feats_in.1, bf16[256,256]{1,0:T(8,128)(2,1)} %w_self_in.1, bf16[256,256]{1,0:T(8,128)(2,1)} %w_neigh_in.1, bf16[8,128,128]{2,1,0:T(8,128)(2,1)} %bitcast.3, ...), custom_call_target="tpu_custom_call" | custom-call | tf_op jit(solution)/shard_map/sage_layer/pallas_call | solution.py:489
  49.3 0.7 %place_results.1 = (bf16[128,256]{1,0:T(8,128)(2,1)}, bf16[128,256]{1,0:T(8,128)(2,1)}, f32[16,256]{1,0:T(8,128)}, f32[16,256]{1,0:T(8,128)}) custom-call(bf16[128,256]{1,0:T(8,128)(2,1)S(1)} %get-tuple-element.8.refs_0_, bf16[128,256]{1,0:T(8,128)(2,1)S(1)} %get-tuple-element.9.refs_1_, f32[16,256]{1,0:T(8,128)S(1)} %get-tuple-element.10.refs_2_, ...), custom_call_target="tpu_custom_call" | custom-call | tf_op jit(solution)/shard_map/place_results/pallas_call | solution.py:508
where the time goes:
time: 50.1 us; the launch traced here: 49.9 us
  Pallas kernels  48.7 us (97%)
  between operations  1.29 us (3%)
    pallas_call x1, Pallas kernels, per_device(): pl.pallas_call(functools.partial(kernel, dims), out_shape=(pltpu.VMEM((T,...  48 us

commit v1 on v0

--- a/solution.py
+++ b/solution.py
@@ -31,8 +31,8 @@
     feats_in, w_self_in, w_neigh_in, tiles_in, owner_in, src_in, count_in, d_out_in,
     out_ref, d_feats_ref, g_self_ref, g_neigh_ref,
     feats_ref, w_self_ref, w_neigh_ref, tiles_ref, owner_ref, src_ref, count_ref, d_out_ref, load_s,
-    panel, dense, dense_sib, dense_t, x_send, x_recv, own, own2, z_send, z_recv, z2_send, z2_recv, x2_send, x2_recv,
-    gather, f_t, m_t, f_in, m_in, w_neigh_t, grad_acc, panel_acc, back_send, back_recv,
+    panel, dense, dense_sib, dense_t, x_send, x_recv, sums_by, z_send, z_recv, z2_send, z2_recv, x2_send, x2_recv,
+    gather, f_t, m_t, row_sums, f_send, f_in, m_in, w_neigh_t, grad_acc, panel_acc, back_send, back_recv,
     gr_send, gr_recv,
     panel_s, panel_r, dense_s, dense_r, xs, xr, zs, zr, z2s, z2r, x2s, x2r, gzs, gzr, gxs, gxr, gcs, gcr,
     fs, fr, ms, mr, bs, br, grs, grr,
@@ -101,6 +101,16 @@
 
         return lax.fori_loop(0, tiles, look, (jnp.int32(0), jnp.int32(0)))
 
+    if small:
+        sums = dot_nt(jnp.ones((EXTRA, T), BF16), tiles_ref[...].reshape(tiles * T, T))
+        for t in range(tiles):
+            row_sums[t] = sums[0:8, t * T:(t + 1) * T]
+    else:
+        def sum_tile(t, _):
+            row_sums[t] = dot_nt(jnp.ones((EXTRA, T), BF16), tiles_ref[t])[0:8]
+            return 0
+        lax.fori_loop(0, tiles, sum_tile, 0)
+
     def build(cc, bb):
         def one(aa, _):
             d = dom_of(aa, bb, cc)
@@ -108,6 +118,10 @@
                 at, live = place(d * R + s)
                 mask = jnp.full((T, T), live.astype(F32), F32).astype(BF16)
                 dense[cc, bb, aa, :, s * T:(s + 1) * T] = tiles_ref[at] * mask
+                part = row_sums[at] * live.astype(F32)
+                deg = part if s == 0 else deg + part
+            high = deg.astype(BF16).astype(F32)
+            f_send[d, chunk:chunk + EXTRA, :] = jnp.concatenate([high, deg - high], axis=0).astype(BF16)
             return 0
         if small:
             for aa in range(A):
@@ -121,6 +135,9 @@
     for cp in loads[4:]:
         cp.wait()
     f_t[...] = feats_ref[...].T
+    for d in range(n_dom):
+        row = d * share // chunk * chunk
+        f_send[d, 0:chunk, :] = f_t[row:row + chunk, :]
     panel[c, pl.ds(pl.multiple_of(rep * T, T), T), :] = feats_ref[...]
 
     pl.semaphore_wait(barrier, n_dom - 1 + 2 * (R - 1))
@@ -148,31 +165,39 @@
         copies.append(cp)
         dense_in[kb] = cp
 
-    def scatter(src, dst, s, r):
+    def chunk_at(d):
+        return pl.ds(pl.multiple_of(lax.div(d * share, chunk) * chunk, chunk), chunk)
+
+    def scatter(pick, dst, s, r):
         for k in range(1, n_dom):
             to = plus(dom, k, n_dom)
-            row = pl.multiple_of(lax.div(to * share, chunk) * chunk, chunk)
-            cp = rcopy(src.at[pl.ds(row, chunk)], dst.at[dom], s.at[k], r.at[k], rep, to)
+            cp = rcopy(pick(to), dst.at[dom], s.at[k], r.at[k], rep, to)
             cp.start()
             copies.append(cp)
-        row = pl.multiple_of(lax.div(dom * share, chunk) * chunk, chunk)
-        dst[dom] = src[pl.ds(row, chunk), :]
-
-    def scatter_wait(src, dst, s, r):
+
+    def scatter_wait(pick, dst, s, r):
         for k in range(1, n_dom):
             frm = plus(dom, n_dom - k, n_dom)
-            rcopy(src.at[pl.ds(0, chunk)], dst.at[frm], s.at[k], r.at[k], rep, frm).wait_recv()
-
-    scatter(f_t, f_in, fs, fr)
+            rcopy(pick(frm), dst.at[frm], s.at[k], r.at[k], rep, frm).wait_recv()
+
+    def pick_f(d):
+        return f_send.at[d]
+
+    def pick_m(d):
+        return m_t.at[chunk_at(d)]
+
     for kb in list(range(1, B)) + [0]:
         build(c, plus(b, kb, B))
-
-    ones = jnp.ones((EXTRA, R * T), BF16)
-
-    def block_sum(bb, aa):
-        top = dot(dense[c, bb, aa], panel[c]) + dot(dense_sib[bb, aa], panel[1 - c])
-        deg = dot_nt(ones, dense[c, bb, aa]) + dot_nt(ones, dense_sib[bb, aa])
-        return top, deg
+    scatter(pick_f, f_in, fs, fr)
+    f_in[dom] = f_send[dom]
+
+    w_neigh_t[...] = w_neigh_ref[...].T
+    pre_self = dot(feats_ref[...], w_self_ref[...])
+    if small:
+        for aa in range(A):
+            for bb in range(B):
+                for cc in range(2):
+                    dense_t[aa, bb, :, cc * T:(cc + 1) * T] = dense[cc, bb, aa].T
 
     def pack(dst, top, row):
         n = top.shape[0]
@@ -184,48 +209,41 @@
     for cp in panel_in:
         cp.wait_recv()
     order = [2, 3, 1, 0] if A == 4 else list(range(1, A)) + [0]
-    for kb in range(B):
+    def block_sums(kb):
+        bb = plus(b, kb, B)
         dense_in[kb].wait_recv()
-    for ka in order:
-        aa = plus(a, ka, A)
-        for kb in list(range(1, B)) + [0]:
-            bb = plus(b, kb, B)
-            top, deg = block_sum(bb, aa)
-            if ka > 0:
-                z2_send[ka, kb * CUT:(kb + 1) * CUT, :] = top[0:CUT].astype(BF16)
-            else:
-                own2[kb] = top[0:CUT]
-            if kb > 0:
-                pack(x_send.at[kb - 1, ka], top[CUT:], deg)
-                i = (kb - 1) * A + ka
-                cp = rcopy(x_send.at[kb - 1, ka], x_recv.at[kb - 1, ka], xs.at[i], xr.at[i], rep,
-                           dom_of(a, bb, c))
-                cp.start()
-                copies.append(cp)
-            else:
-                own[ka, 0:T - CUT, :] = top[CUT:]
-                own[ka, T - CUT:T - CUT + EXTRA, 0:T] = deg
-        if ka > 0:
-            cp = rcopy(z2_send.at[ka], z2_recv.at[ka], z2s.at[ka], z2r.at[ka], rep, dom_of(aa, b, c))
+        res = dot(dense[c, bb].reshape(A * T, R * T), panel[c])
+        res = res + dot(dense_sib[bb].reshape(A * T, R * T), panel[1 - c])
+        sums_by[kb] = res.reshape(A, T, hid)
+
+    for kb in range(1, B):
+        block_sums(kb)
+        for ka in order:
+            x_send[kb - 1, ka] = sums_by[kb, plus(a, ka, A), CUT:T].astype(BF16)
+            i = (kb - 1) * A + ka
+            cp = rcopy(x_send.at[kb - 1, ka], x_recv.at[kb - 1, ka], xs.at[i], xr.at[i], rep,
+                       dom_of(a, plus(b, kb, B), c))
             cp.start()
             copies.append(cp)
-
-    low = T - CUT
+    block_sums(0)
+    for ka in order[:-1]:
+        aa = plus(a, ka, A)
+        for kb in range(B):
+            z2_send[ka, kb * CUT:(kb + 1) * CUT, :] = sums_by[kb, aa, 0:CUT].astype(BF16)
+        cp = rcopy(z2_send.at[ka], z2_recv.at[ka], z2s.at[ka], z2r.at[ka], rep, dom_of(aa, b, c))
+        cp.start()
+        copies.append(cp)
 
     def with_x(ka):
-        top = own[ka, 0:low, :]
-        deg = own[ka, low:low + EXTRA, 0:T]
+        top = sums_by[0, plus(a, ka, A), CUT:T]
         for kb in range(1, B):
             i = (kb - 1) * A + ka
             rcopy(x_send.at[kb - 1, ka], x_recv.at[kb - 1, ka], xs.at[i], xr.at[i], rep, sib).wait_recv()
-            got = x_recv[kb - 1, ka].astype(F32)
-            top = top + got[0:low]
-            deg = deg + got[low:, 0:T] + got[low:, T:2 * T]
-        return top, deg
+            top = top + x_recv[kb - 1, ka].astype(F32)
+        return top
 
     for ka in order[:-1]:
-        top, deg = with_x(ka)
-        pack(z_send.at[ka], top, deg)
+        z_send[ka] = with_x(ka).astype(BF16)
         cp = rcopy(z_send.at[ka], z_recv.at[ka], zs.at[ka], zr.at[ka], rep,
                    dom_of(plus(a, ka, A), b, c))
         cp.start()
@@ -233,7 +251,7 @@
     for ka in order[:-1]:
         rcopy(z2_send.at[ka], z2_recv.at[ka], z2s.at[ka], z2r.at[ka], rep, sib).wait_recv()
     for kb in list(range(1, B)) + [0]:
-        part = own2[kb]
+        part = sums_by[kb, a, 0:CUT]
         for ka in range(1, A):
             part = part + z2_recv[ka, kb * CUT:(kb + 1) * CUT, :].astype(F32)
         if kb > 0:
@@ -243,33 +261,29 @@
             cp.start()
             copies.append(cp)
     head = part
-
-    w_neigh_t[...] = w_neigh_ref[...].T
-    pre_self = dot(feats_ref[...], w_self_ref[...])
-    if small:
-        for aa in range(A):
-            for bb in range(B):
-                for cc in range(2):
-                    dense_t[aa, bb, :, cc * T:(cc + 1) * T] = dense[cc, bb, aa].T
-
-    top, deg = with_x(0)
+    scatter_wait(pick_f, f_in, fs, fr)
+    deg = f_in[0, chunk:chunk + EXTRA].astype(F32)
+    for k in range(1, n_dom):
+        deg = deg + f_in[k, chunk:chunk + EXTRA].astype(F32)
+    inv = 1.0 / (1.0 + (deg[0:8] + deg[8:16]))
+    inv = jnp.concatenate([inv, inv], axis=0)
+
+    def as_column(row):
+        col = jnp.broadcast_to(row[0:1, :], (T, T)).T
+        return jnp.concatenate([col] * (hid // T), axis=1)
+
+    inv_col = as_column(inv)
+
+    top = with_x(0)
     for ka in order[:-1]:
         rcopy(z_send.at[ka], z_recv.at[ka], zs.at[ka], zr.at[ka], rep, sib).wait_recv()
-        got = z_recv[ka].astype(F32)
-        top = top + got[0:low]
-        deg = deg + got[low:, 0:T] + got[low:, T:2 * T]
+        top = top + z_recv[ka].astype(F32)
     for kb in range(1, B):
         rcopy(x2_send.at[kb], x2_recv.at[kb], x2s.at[kb], x2r.at[kb], rep, sib).wait_recv()
         head = head + x2_recv[kb].astype(F32)
     top = jnp.concatenate([head, top], axis=0)
 
-    inv = 1.0 / (1.0 + deg)
-
-    def as_column(row):
-        col = jnp.broadcast_to(row[0:1, :], (T, T)).T
-        return jnp.concatenate([col] * (hid // T), axis=1)
-
-    mean = (top * as_column(inv)).astype(BF16)
+    mean = (top * inv_col).astype(BF16)
     pre = pre_self + dot(mean, w_neigh_ref[...])
     g = jax.nn.sigmoid(pre)
     d_pre = (d_out_ref[...].astype(F32) * g * (1.0 + pre * (1.0 - g))).astype(BF16)
@@ -312,38 +326,46 @@
         ec.wait_send()
     panel_acc[...] = jnp.zeros_like(panel_acc)
     grad_acc[...] = jnp.zeros_like(grad_acc)
-    scatter(m_t, m_in, ms, mr)
-
-    def wait_c(ka, kb):
-        blk = block_at(ka, kb, 1 - c)
-        i = kb * A + ka
-        rcopy(blk, blk, gcs.at[i], gcr.at[i], rep, sib).wait_recv()
-
-    def use_pair(ka, kb):
-        wait_c(ka, kb)
-        aa, bb = plus(a, A - ka, A), plus(b, B - kb, B)
-        d = [gather[aa, bb, cc, 0:T, :] for cc in range(2)]
-        both = jnp.concatenate(d, axis=0)
-        cols = []
-        for cc in range(2):
-            row = gather[aa, bb, cc, T:T + EXTRA, :].astype(F32)
-            cols.append(as_column(row[:, 0:T] + row[:, T:2 * T]))
-        d_sum = (dot(both, w_neigh_t[...]) * jnp.concatenate(cols, axis=0)).astype(BF16)
+    scatter(pick_m, m_in, ms, mr)
+    m_in[dom] = m_t[chunk_at(dom), :]
+
+    def use(ka, kbs):
+        d, cols, lhs = [], [], []
+        aa = plus(a, A - ka, A)
+        for kb in kbs:
+            bb = plus(b, B - kb, B)
+            blk = block_at(ka, kb, 1 - c)
+            i = kb * A + ka
+            rcopy(blk, blk, gcs.at[i], gcr.at[i], rep, sib).wait_recv()
+            for cc in range(2):
+                d.append(gather[aa, bb, cc, 0:T, :])
+                row = gather[aa, bb, cc, T:T + EXTRA, :].astype(F32)
+                cols.append(as_column(row[:, 0:T] + row[:, T:2 * T]))
+            if small:
+                lhs.append(dense_t[aa, bb])
+        d_sum = dot(jnp.concatenate(d, axis=0), w_neigh_t[...]) * jnp.concatenate(cols, axis=0)
+        d_sum = d_sum.astype(BF16)
         if small:
-            panel_acc[...] += dot(dense_t[aa, bb], d_sum)
-        else:
+            panel_acc[...] += dot(jnp.concatenate(lhs, axis=1), d_sum)
+            return
+        for n, kb in enumerate(kbs):
+            bb = plus(b, B - kb, B)
             for cc in range(2):
+                at = (n * 2 + cc) * T
                 for s in range(R):
                     panel_acc[s * T:(s + 1) * T, :] += dot_tn(
-                        dense[cc, bb, aa, :, s * T:(s + 1) * T], d_sum[cc * T:(cc + 1) * T]
+                        dense[cc, bb, aa, :, s * T:(s + 1) * T], d_sum[at:at + T]
                     )
 
-    def grads_of(ka, kb):
-        aa, bb = plus(a, A - ka, A), plus(b, B - kb, B)
-        first = dom_of(aa, bb, 0)
-        lhs = [jnp.concatenate([r[first], r[first + 1]], axis=1) for r in (f_in, m_in)]
-        rhs = jnp.concatenate([gather[aa, bb, cc, 0:T, :] for cc in range(2)], axis=0)
-        grad_acc[...] += dot(jnp.concatenate(lhs, axis=0), rhs)
+    def grads_of(pairs):
+        lhs, rhs = [], []
+        for ka, kb in pairs:
+            aa, bb = plus(a, A - ka, A), plus(b, B - kb, B)
+            for cc in range(2):
+                at = dom_of(aa, bb, cc)
+                lhs.append(jnp.concatenate([f_in[at, 0:chunk], m_in[at]], axis=0))
+                rhs.append(gather[aa, bb, cc, 0:T, :])
+        grad_acc[...] += dot(jnp.concatenate(lhs, axis=1), jnp.concatenate(rhs, axis=0))
 
     done = []
     later = []
@@ -358,18 +380,16 @@
             i = kb * A + ka
             rcopy(blk, blk, gxs.at[i], gxr.at[i], rep, sib).wait_recv()
             send_c(ka, kb)
-        for pair in later:
-            use_pair(*pair)
+        if later:
+            use(later[0][0], [kb for _, kb in later])
         done += later
         later = [(ka, kb) for kb in range(B)]
-    use_pair(*later[0])
+    use(later[0][0], [later[0][1]])
     done.append(later.pop(0))
-    scatter_wait(f_t, f_in, fs, fr)
-    scatter_wait(m_t, m_in, ms, mr)
-    for pair in done:
-        grads_of(*pair)
-    for pair in later:
-        use_pair(*pair)
+    scatter_wait(pick_m, m_in, ms, mr)
+    grads_of(done)
+    for ka, kb in later:
+        use(ka, [kb])
 
     back = []
     for kr in range(1, R):
@@ -379,8 +399,8 @@
         cp = rcopy(back_send.at[kr], back_recv.at[kr], bs.at[kr], br.at[kr], to, dom)
         cp.start()
         back.append(cp)
-    for pair in later:
-        grads_of(*pair)
+    if later:
+        grads_of(later)
     gr_send[...] = grad_acc[...]
     for kr in range(1, R):
         cp = rcopy(gr_send, gr_recv.at[kr], grs.at[kr], grr.at[kr], plus(rep, kr, R), dom)
@@ -450,12 +470,11 @@
         pltpu.VMEM((2, B, A, T, R * T), BF16),
         pltpu.VMEM((B, A, T, R * T), BF16),
         pltpu.VMEM((A, B, R * T, 2 * T) if small else (1, 1, 16, 128), BF16),
-        pltpu.VMEM((B - 1, A, msg - CUT, hid), BF16),
-        pltpu.VMEM((B - 1, A, msg - CUT, hid), BF16),
-        pltpu.VMEM((A, msg - CUT, hid), F32),
-        pltpu.VMEM((B, CUT, hid), F32),
-        pltpu.VMEM((A, msg - CUT, hid), BF16),
-        pltpu.VMEM((A, msg - CUT, hid), BF16),
+        pltpu.VMEM((B - 1, A, T - CUT, hid), BF16),
+        pltpu.VMEM((B - 1, A, T - CUT, hid), BF16),
+        pltpu.VMEM((B, A, T, hid), F32),
+        pltpu.VMEM((A, T - CUT, hid), BF16),
+        pltpu.VMEM((A, T - CUT, hid), BF16),
         pltpu.VMEM((A, B * CUT, hid), BF16),
         pltpu.VMEM((A, B * CUT, hid), BF16),
         pltpu.VMEM((B, CUT, hid), BF16),
@@ -463,7 +482,9 @@
         pltpu.VMEM((A, B, 2, msg, hid), BF16),
         pltpu.VMEM((hid, T), BF16),
         pltpu.VMEM((hid, T), BF16),
-        pltpu.VMEM((n_dom, chunk, T), BF16),
+        pltpu.VMEM((tiles, 8, T), F32),
+        pltpu.VMEM((n_dom, chunk + EXTRA, T), BF16),
+        pltpu.VMEM((n_dom, chunk + EXTRA, T), BF16),
         pltpu.VMEM((n_dom, chunk, T), BF16),
         pltpu.VMEM((hid, hid), BF16),
         pltpu.VMEM((2 * chunk, hid), F32),

time: 50.1 us -> 50.6 us (level)
  no operation moved by 1% of the time
where the time goes in v1:
time: 50.6 us; the launch traced here: 50.4 us
  Pallas kernels  49.1 us (97%)
  between operations  1.29 us (3%)
    pallas_call x1, Pallas kernels, per_device(): pl.pallas_call(functools.partial(kernel, dims), out_shape=(pltpu.VMEM((T,...  48.4 us

profile of v1, /device:TPU:0, one launch (start us, length us, event | category | flops | bytes accessed | tf_op | source)
XLA Modules:
  0.0 50.4 jit_solution(8267157527374157733)
XLA Ops:
  1.3 48.4 %sage_layer.1 = (bf16[128,256]{1,0:T(8,128)(2,1)S(1)}, bf16[128,256]{1,0:T(8,128)(2,1)S(1)}, f32[16,256]{1,0:T(8,128)S(1)}, f32[16,256]{1,0:T(8,128)S(1)}) custom-call(bf16[128,256]{1,0:T(8,128)(2,1)} %feats_in.1, bf16[256,256]{1,0:T(8,128)(2,1)} %w_self_in.1, bf16[256,256]{1,0:T(8,128)(2,1)} %w_neigh_in.1, bf16[8,128,128]{2,1,0:T(8,128)(2,1)} %bitcast.3, ...), custom_call_target="tpu_custom_call" | custom-call | tf_op jit(solution)/shard_map/sage_layer/pallas_call | solution.py:510
  49.7 0.7 %place_results.1 = (bf16[128,256]{1,0:T(8,128)(2,1)}, bf16[128,256]{1,0:T(8,128)(2,1)}, f32[16,256]{1,0:T(8,128)}, f32[16,256]{1,0:T(8,128)}) custom-call(bf16[128,256]{1,0:T(8,128)(2,1)S(1)} %get-tuple-element.8.refs_0_, bf16[128,256]{1,0:T(8,128)(2,1)S(1)} %get-tuple-element.9.refs_1_, f32[16,256]{1,0:T(8,128)S(1)} %get-tuple-element.10.refs_2_, ...), custom_call_target="tpu_custom_call" | custom-call | tf_op jit(solution)/shard_map/place_results/pallas_call | solution.py:529
